TPU v7x, 128 devices: a whole 4x4x4 slice. The times are simulated.
128 devices in a mesh: span: 4 (over z), stream: 32 (over y, x, core).
Axes of the slice: x: 4, y: 4, z: 4, core: 2. Of those that a mesh axis runs over, the one named last changes fastest.
Arguments:
- conserved_vector: float32 [5, 16, 512, 512], P(None, 'span', 'stream'), may hold values from -1 to 4, as said below
- occupied_patches: int32 [128], P(('span', 'stream')), may hold values from 0 to 8, as said below
- reading_volume: int32 [128, 128, 8], P(('span', 'stream')), may hold values from 0 to 32767, as said below
- reading_surface: int32 [128, 128, 8], P(('span', 'stream')), may hold values from -1 to 1023, as said below
- reading_elevation: float32 [131072], P(('span', 'stream')), may hold values from 0.5 to 2
- airfoil_surface_kelvin: float32 [131072], P(('span', 'stream')), may hold values from 0.5 to 0.9
Outputs:
- new_field: float32 [5, 16, 512, 512], P(None, 'span', 'stream')
- wall_flux: float32 [2, 131072], P(None, ('span', 'stream'))
Inputs may be any that keep to these rules, and one draw needn't show every extreme that they name: `conserved_vector`: density 0.8 to 1.2, streamwise velocity 0.25 to 0.55, radial and pitchwise velocities within 0.15 in magnitude, pressure 0.8 to 1.2, energy = pressure / 0.4 plus half density times speed squared. The live faces of a device are its first 128 * occupied_patches ones; some device is full in every draw. `reading_volume`: a local cell number of the source's block. `reading_surface`: -1 marks an empty slot; each live face of the receiver appears exactly once over all sources and slots, no other face appears; a full receiver fills all 8 slots from every source.
All inputs are finite; a program needn't handle non-finite values.
Results may differ from a plain program's by a relative error of at most 0.0001.
Values sent between devices are 32-bit elements; how exact they have to be, the bound alone decides.
No kernel may reach another device: no remote copies, remote signals or barrier semaphores. Data moves between devices by JAX's collectives and lax.ppermute only.
A program may use at most 64 MiB of HBM per device.

v0:
```python
import math

import jax
import jax.numpy as jnp
import numpy as np
from jax import lax
from jax.experimental import pallas as pl
from jax.experimental.pallas import tpu as pltpu
from jax.sharding import PartitionSpec as P

NPTS = 64
ITERS = 6
HALO = 3
LANES = 128
QUARTERS = 4
LIMIT_INNER = 12 * 2**20
LIMIT_FIELD = 24 * 2**20
ROWS = 40

f32 = jnp.float32
bf16 = jnp.bfloat16


def split_bf16(x, parts):
    out = []
    for _ in range(parts):
        out.append(x.astype(bf16))
        x = x - out[-1].astype(f32)
    return out


def gather_kernel(view, cells, out, table, halves):
    for c in range(5):
        rows = [jnp.concatenate([view[c, a, j] for j in range(QUARTERS)], axis=1) for a in range(4)]
        put_halves(halves, c, jnp.concatenate(rows, axis=0))
    table[...] = jnp.zeros((LANES, LANES), f32)
    pitch_of = lax.broadcasted_iota(jnp.int32, (512, LANES), 0)
    row_of = lax.broadcasted_iota(jnp.int32, (64, LANES), 0)

    def pair(n, _):
        slots = [cells[pl.ds(2 * n + k, 1), :] for k in range(2)]
        hot = jnp.concatenate(
            [
                jnp.where(pitch_of == ((cell & 3) << 7) + ((cell & 511) >> 2), 1.0, 0.0).astype(bf16)
                for cell in slots
            ],
            axis=1,
        )
        got = lax.dot_general(
            halves[...], hot, (((1,), (0,)), ((), ())), preferred_element_type=f32
        )
        for k, cell in enumerate(slots):
            here = row_of == (cell >> 9)
            for c in range(5):
                lanes = slice(k * LANES, (k + 1) * LANES)
                both = got[c * 64 : c * 64 + 64, lanes] + got[320 + c * 64 : 384 + c * 64, lanes]
                table[pl.ds(c * 8 + 2 * n + k, 1), :] = jnp.sum(
                    jnp.where(here, both, 0.0), axis=0, keepdims=True
                )
        return 0

    lax.fori_loop(0, 4, pair, 0)
    out[...] = jnp.transpose(table[...])


def gather_samples(view, volume):
    return pl.pallas_call(
        gather_kernel,
        out_shape=jax.ShapeDtypeStruct((LANES, LANES), f32),
        in_specs=[pl.BlockSpec(memory_space=pltpu.VMEM)] * 2,
        out_specs=pl.BlockSpec(memory_space=pltpu.VMEM),
        scratch_shapes=[
            pltpu.VMEM((LANES, LANES), f32),
            pltpu.VMEM((640, 512), bf16),
        ],
        compiler_params=pltpu.CompilerParams(vmem_limit_bytes=40 * 2**20),
        cost_estimate=pl.CostEstimate(flops=10**9, bytes_accessed=10**6, transcendentals=0),
    )(view, volume)


_levels = np.exp(3.0 * np.arange(NPTS) / (NPTS - 1)) - 1.0
_levels = _levels / (math.exp(3.0) - 1.0)
_spacing = [float(v) for v in _levels[1:] - _levels[:-1]]
_middle = [float(v) for v in 0.5 * (_levels[1:] + _levels[:-1])]


def face_kernel(tiles, surface, height, kelvin, hot, tile_of, live, h, wall):
    by_slot = surface[...]
    tall = jnp.concatenate([by_slot, jnp.zeros((LANES - 8, LANES), jnp.int32)], axis=0)
    low_bits = jnp.transpose(tall.astype(f32)).astype(jnp.int32) & 127
    lane = lax.broadcasted_iota(jnp.int32, (LANES, LANES), 1)
    for k in range(8):
        hot[pl.ds(k * LANES, LANES), :] = jnp.where(lane == low_bits[:, k : k + 1], 1.0, 0.0).astype(bf16)
    tile_of[...] = jnp.where(by_slot < 0, -1, by_slot >> 7)
    live[...] = jnp.where(lax.broadcasted_iota(jnp.int32, (8, LANES), 0) < tiles[0], 1.0, 0.0)
    h[...] = height[...]
    wall[...] = kelvin[...]


def face_tables(tiles, surface, height, kelvin):
    tile = jax.ShapeDtypeStruct((8, LANES), f32)
    return pl.pallas_call(
        face_kernel,
        out_shape=(
            jax.ShapeDtypeStruct((8 * LANES, LANES), bf16),
            jax.ShapeDtypeStruct((8, LANES), jnp.int32),
            tile,
            tile,
            tile,
        ),
        in_specs=[pl.BlockSpec(memory_space=pltpu.SMEM)]
        + [pl.BlockSpec(memory_space=pltpu.VMEM)] * 3,
        out_specs=(pl.BlockSpec(memory_space=pltpu.VMEM),) * 5,
        compiler_params=pltpu.CompilerParams(vmem_limit_bytes=40 * 2**20),
        cost_estimate=pl.CostEstimate(flops=10**6, bytes_accessed=10**6, transcendentals=0),
    )(tiles, surface, height, kelvin)


def wall_kernel(received, hot, tile_of, alive, height, kelvin, _mark, out):
    table = jnp.transpose(received[...])
    sub = lax.broadcasted_iota(jnp.int32, (8, LANES), 0)
    here = [sub == tile_of[k : k + 1] for k in range(8)]
    spread = jnp.concatenate(
        [
            jnp.concatenate(
                [jnp.where(here[k], table[c * 8 + k : c * 8 + k + 1], 0.0) for k in range(8)], axis=1
            )
            for c in range(5)
        ],
        axis=0,
    )
    parts = jnp.concatenate(split_bf16(spread, 2), axis=0)
    faces = lax.dot_general(parts, hot[...], (((1,), (0,)), ((), ())), preferred_element_type=f32)
    faces = faces[40:] + faces[:40]
    live = alive[...] > 0.5
    filler = (1.0, 0.4, 0.0, 0.0, 3.0)
    rho, mx, my, mz, energy = (
        jnp.where(live, faces[c * 8 : c * 8 + 8], filler[c]) for c in range(5)
    )
    h = height[...]
    wall = kelvin[...]
    power = mx * mx + my * my + mz * mz
    speed = jnp.sqrt(power) / rho
    temperature = 0.4 * (energy - 0.5 * power / rho) / rho
    tau = 0.002 * speed / h

    def inverse(x):
        return pl.reciprocal(x, approx=True)

    def viscosity(tau):
        friction = jnp.sqrt(tau / rho)
        a = rho * 0.41 * friction * h
        b = friction * rho * h * (-math.log2(math.e) / (0.002 * 17.0))
        return a, b

    def eddy(a, b, j):
        damp = 1.0 - jnp.exp2(b * _middle[j])
        return (a * _middle[j]) * (damp * damp)

    def step(_, tau):
        a, b = viscosity(tau)
        total = [jnp.zeros_like(tau) for _ in range(4)]
        for j in range(NPTS - 1):
            total[j % 4] = total[j % 4] + _spacing[j] * inverse(0.002 + eddy(a, b, j))
        total = (total[0] + total[1]) + (total[2] + total[3])
        return tau * speed / (tau * h * total)

    tau = lax.fori_loop(0, ITERS - 1, step, tau)
    a, b = viscosity(tau)
    total = jnp.zeros_like(tau)
    impedance = jnp.zeros_like(tau)
    work = jnp.zeros_like(tau)
    for j in range(NPTS - 1):
        nu = eddy(a, b, j)
        increment = _spacing[j] * inverse(0.002 + nu)
        total = total + increment
        part = _spacing[j] * inverse(3.5 * (0.002 / 0.72) + (3.5 / 0.9) * nu)
        impedance = impedance + part
        work = work + (total - 0.5 * increment) * part
    scale = tau * h
    rate = (temperature - wall + tau * (scale * h * work)) / (h * impedance)
    tau = tau * speed / (scale * total)
    friction = jnp.where(live, 100.0 * tau / (rho * speed * speed), 0.0)
    heat = jnp.where(live, 100.0 * rate / (rho * 3.5 * speed), 0.0)
    for i in range(8):
        out[0:1, i * LANES : (i + 1) * LANES] = friction[i : i + 1]
        out[1:2, i * LANES : (i + 1) * LANES] = heat[i : i + 1]


def wall_faces(received, tables, mark):
    return pl.pallas_call(
        wall_kernel,
        out_shape=jax.ShapeDtypeStruct((2, 8 * LANES), f32),
        in_specs=[pl.BlockSpec(memory_space=pltpu.VMEM)] * 6 + [pl.BlockSpec(memory_space=pl.ANY)],
        out_specs=pl.BlockSpec(memory_space=pltpu.VMEM),
        compiler_params=pltpu.CompilerParams(vmem_limit_bytes=40 * 2**20),
        cost_estimate=pl.CostEstimate(flops=10**8, bytes_accessed=10**6, transcendentals=10**6),
    )(received, *tables, mark)


def pitch_map(across):
    p = lax.broadcasted_iota(jnp.int32, (512, 512), 1 if across else 0)
    n = lax.broadcasted_iota(jnp.int32, (512, 512), 0 if across else 1)
    return jnp.where(p == 4 * (n & 127) + (n >> 7), 1.0, 0.0).astype(bf16)


def put_halves(halves, c, rows):
    hi, low = split_bf16(rows, 2)
    halves[pl.ds(c * 64, 64), :] = hi
    halves[pl.ds(320 + c * 64, 64), :] = low


def remap(halves, table):
    got = lax.dot_general(halves[...], table, (((1,), (0,)), ((), ())), preferred_element_type=f32)
    return got[:320] + got[320:]


def view_kernel(state, view, first, second, raw, halves, sems):
    copies = [
        [pltpu.make_async_copy(state.at[c, a], raw.at[c, a], sems.at[4 * c + a]) for a in range(4)]
        for c in range(5)
    ]
    for c in range(5):
        for copy in copies[c]:
            copy.start()
    table = pitch_map(False)
    odd = lax.axis_index("stream") % 2
    row_first = (1 - odd) * (16 - HALO)
    row_second = odd * (16 - HALO)
    for c in range(5):
        for copy in copies[c]:
            copy.wait()
        put_halves(halves, c, raw[c].reshape(64, 512))
    x = remap(halves, table)
    for c in range(5):
        for a in range(4):
            for j in range(QUARTERS):
                at = 64 * c + 16 * a
                view[c, a, j] = x[at : at + 16, j * LANES : (j + 1) * LANES]
    for c in range(5):
        for a in range(4):
            for j in range(QUARTERS):
                at = ((c * 4 + a) * QUARTERS + j) * HALO
                first[pl.ds(at, HALO), :] = view[c, a, j, pl.ds(row_first, HALO), :]
                second[pl.ds(at, HALO), :] = view[c, a, j, pl.ds(row_second, HALO), :]


def view_field(state):
    side = jax.ShapeDtypeStruct((5 * 4 * QUARTERS * HALO, LANES), f32)
    return pl.pallas_call(
        view_kernel,
        out_shape=(jax.ShapeDtypeStruct((5, 4, QUARTERS, 16, LANES), f32), side, side),
        in_specs=[pl.BlockSpec(memory_space=pltpu.HBM)],
        out_specs=(pl.BlockSpec(memory_space=pltpu.VMEM),) * 3,
        scratch_shapes=[
            pltpu.VMEM((5, 4, 16, 512), f32),
            pltpu.VMEM((640, 512), bf16),
            pltpu.SemaphoreType.DMA((20,)),
        ],
        compiler_params=pltpu.CompilerParams(vmem_limit_bytes=40 * 2**20),
        cost_estimate=pl.CostEstimate(flops=10**9, bytes_accessed=3 * 10**6, transcendentals=0),
    )(pltpu.with_memory_space_constraint(state, pltpu.HBM))


REACH = ((1, -2, 20, 0), (2, -1, 18, 20), (3, 0, 16, 38))
SIDE = 54


def pack_kernel(view, stream_b, stream_a, _samples, first, second):
    span_odd = lax.axis_index("span") % 2
    stream_odd = lax.axis_index("stream") % 2

    def fill(before, after):
        def body(c, _):
            for out, high in ((first, span_odd == 0), (second, span_odd == 1)):
                for distance, _, count, base in REACH:
                    plane = jnp.where(high, 4 - distance, distance - 1)
                    extra = HALO - distance
                    for j in range(QUARTERS):
                        at = (c * QUARTERS + j) * SIDE + base
                        side = ((c * 4 + plane) * QUARTERS + j) * HALO
                        for i in range(2):
                            out[pl.ds(at + extra + 8 * i, 8), :] = view[c, plane, j, pl.ds(8 * i, 8), :]
                        if extra:
                            out[pl.ds(at, extra), :] = before[pl.ds(side + distance, extra), :]
                            out[pl.ds(at + extra + 16, extra), :] = after[pl.ds(side, extra), :]
            return 0

        lax.fori_loop(0, 5, body, 0)

    @pl.when(stream_odd == 0)
    def _():
        fill(stream_b, stream_a)

    @pl.when(stream_odd == 1)
    def _():
        fill(stream_a, stream_b)


def pack_planes(view, stream_b, stream_a, samples):
    shape = jax.ShapeDtypeStruct((5 * QUARTERS * SIDE, LANES), f32)
    return pl.pallas_call(
        pack_kernel,
        out_shape=(shape, shape),
        in_specs=[pl.BlockSpec(memory_space=pltpu.VMEM)] * 3 + [pl.BlockSpec(memory_space=pl.ANY)],
        out_specs=(pl.BlockSpec(memory_space=pltpu.VMEM),) * 2,
        compiler_params=pltpu.CompilerParams(vmem_limit_bytes=40 * 2**20),
        cost_estimate=pl.CostEstimate(flops=10**6, bytes_accessed=2 * 10**6, transcendentals=0),
    )(view, stream_b, stream_a, samples)


def swap(x, axis, parity):
    spans, streams = lax.axis_size("span"), lax.axis_size("stream")

    def partner(i, n):
        other = i + 1 if i % 2 == parity else i - 1
        return other if 0 <= other < n else None

    pairs = []
    for a in range(spans):
        for b in range(streams):
            if axis == "span":
                other = partner(a, spans)
                there = (a, b ^ 1) if other is None else (other, b)
            else:
                other = partner(b, streams)
                there = (a ^ 1, b) if other is None else (a, other)
            pairs.append((a * streams + b, there[0] * streams + there[1]))
    return lax.ppermute(x, ("span", "stream"), pairs)


NORMAL = ((0, 1, 2, 6), (1, 3, 4, 7), (2, 4, 5, 8))
MIDDLE = (HALO, HALO + 8)


def chunks_from(row):
    return tuple(row - 1 + 8 * i for i in range(3))


def primitive(u):
    rho, m1, m2, m3, energy = u
    inv = pl.reciprocal(rho, approx=True)

    v1, v2, v3 = m1 * inv, m2 * inv, m3 * inv
    t11, t22, t33 = m1 * v1, m2 * v2, m3 * v3
    pressure = 0.4 * energy - 0.2 * (t11 + t22 + t33)
    total = energy + pressure
    square = 1.4 * pressure * inv
    sound = square * lax.rsqrt(square) + 0.04
    return [
        t11 + pressure,
        m1 * v2,
        m1 * v3,
        t22 + pressure,
        m2 * v3,
        t33 + pressure,
        total * v1,
        total * v2,
        total * v3,
        jnp.abs(v1) + sound,
        jnp.abs(v2) + sound,
        jnp.abs(v3) + sound,
    ]


def after(x):
    return jnp.concatenate([x[1:], pltpu.roll(x[:1], LANES - 1, 2)], axis=0)


def before(x):
    return jnp.concatenate([pltpu.roll(x[-1:], 1, 2), x[:-1]], axis=0)


def stage_tools(src, der, gspan, gstream, finish):
    def fill(p, rows):
        for r in rows:
            at = pl.ds(r, 8)
            for n, d in enumerate(primitive([src[c, p, :, at, :] for c in range(5)])):
                der[n, p, :, at, :] = d

    def flux(c, k, p, at):
        return src[1 + k, p, :, at, :] if c == 0 else der[NORMAL[k][c - 1], p, :, at, :]

    def span_faces(p, rows, slot):
        for r in rows:
            at = pl.ds(r, 8)
            coef = jnp.maximum(der[9, p, :, at, :], der[9, p + 1, :, at, :])
            for c in range(5):
                g = (coef - 0.04 if c == 0 else coef) * (src[c, p + 1, :, at, :] - src[c, p, :, at, :])
                gspan[slot, c, :, at, :] = g - (flux(c, 0, p, at) + flux(c, 0, p + 1, at))

    def outputs(p, rows, whole, low_slot, high_slot, faces):
        for i, r in enumerate(rows):
            at, up, down = pl.ds(r, 8), pl.ds(r + 1, 8), pl.ds(r - 1, 8)
            here = der[11, p, :, at, :]
            stream_wave = der[10, p, :, at, :]
            coef_stream = jnp.maximum(stream_wave, der[10, p, :, up, :])
            coef_pitch = jnp.maximum(here, after(here))
            direct = whole and i == 0
            if direct:
                coef_down = jnp.maximum(stream_wave, der[10, p, :, down, :])
            if faces:
                coef_span = jnp.maximum(der[9, p, :, at, :], der[9, p + 1, :, at, :])
            for c in range(5):

                def weigh(coef):
                    return coef - 0.04 if c == 0 else coef

                u = src[c, p, :, at, :]
                if faces:
                    g = weigh(coef_span) * (src[c, p + 1, :, at, :] - u)
                    g = g - (flux(c, 0, p, at) + flux(c, 0, p + 1, at))
                    gspan[high_slot, c, :, at, :] = g
                else:
                    g = gspan[high_slot, c, :, at, :]
                acc = g - gspan[low_slot, c, :, at, :]
                f = flux(c, 1, p, at)
                g = weigh(coef_stream) * (src[c, p, :, up, :] - u) - (f + flux(c, 1, p, up))
                gstream[c, :, pl.ds(r + 8, 8), :] = g
                if direct:
                    low = weigh(coef_down) * (u - src[c, p, :, down, :]) - (f + flux(c, 1, p, down))
                else:
                    low = gstream[c, :, pl.ds(r + 7, 8), :]
                acc = acc + (g - low)
                f = flux(c, 2, p, at)
                h = weigh(coef_pitch) * (after(u) - u) - (f + after(f))
                finish(c, p, r, i, u, acc + (h - before(h)))

    return fill, span_faces, outputs


def clamp_planes(e):
    at = lax.axis_index("span")

    def copy(dst, src):
        for c in range(5):
            for i in range(3):
                e[c, dst, :, pl.ds(8 * i, 8), :] = e[c, src, :, pl.ds(8 * i, 8), :]

    @pl.when(at == 0)
    def _():
        copy(2, 3)

    @pl.when(at == lax.axis_size("span") - 1)
    def _():
        copy(7, 6)


def clamp_rows(e, planes):
    at = lax.axis_index("stream")

    def copy(dst, src):
        for c in range(5):
            for p in planes:
                for q in range(QUARTERS):
                    e[c, p, q, pl.ds(dst, 1), :] = e[c, p, q, pl.ds(src, 1), :]

    @pl.when(at == 0)
    def _():
        copy(2, 3)

    @pl.when(at == lax.axis_size("stream") - 1)
    def _():
        copy(19, 18)


def first_stage(e0, e1):
    def finish(c, p, r, i, u, acc):
        e1[c, p, :, pl.ds(r, 8), :] = u + 0.05 * acc

    return finish


def inner_kernel(view, stream_a, stream_b, e0, e1, der, table, gspan, gstream):
    odd = lax.axis_index("stream") % 2

    def own(c, _):
        for p in range(4):
            for i in range(2):
                e0[c, HALO + p, :, pl.ds(HALO + 8 * i, 8), :] = view[c, p, :, pl.ds(8 * i, 8), :]
        return 0

    lax.fori_loop(0, 5, own, 0)

    def halo_rows(before, after):
        def body(c, _):
            for p in range(4):
                for j in range(QUARTERS):
                    at = ((c * 4 + p) * QUARTERS + j) * HALO
                    e0[c, HALO + p, j, pl.ds(0, HALO), :] = before[pl.ds(at, HALO), :]
                    e0[c, HALO + p, j, pl.ds(HALO + 16, HALO), :] = after[pl.ds(at, HALO), :]
            return 0

        lax.fori_loop(0, 5, body, 0)

    @pl.when(odd == 0)
    def _():
        halo_rows(stream_b, stream_a)

    @pl.when(odd == 1)
    def _():
        halo_rows(stream_a, stream_b)

    clamp_rows(e0, range(3, 7))
    fill, span_faces, outputs = stage_tools(e0, der, gspan, gstream, first_stage(e0, e1))
    wide = chunks_from(1)

    def prims(p, _):
        fill(p, wide)
        return 0

    lax.fori_loop(3, 7, prims, 0)
    span_faces(3, wide, 1)

    def plane(p, _):
        outputs(p, wide, False, 1 - (p & 1), p & 1, True)
        return 0

    lax.fori_loop(4, 6, plane, 0)
    table[...] = pitch_map(True)


def inner_planes(view, stream_a, stream_b):
    block = jax.ShapeDtypeStruct((5, 10, QUARTERS, ROWS, LANES), f32)
    return pl.pallas_call(
        inner_kernel,
        out_shape=(
            block,
            block,
            jax.ShapeDtypeStruct((12, 10, QUARTERS, ROWS, LANES), f32),
            jax.ShapeDtypeStruct((512, 512), bf16),
        ),
        in_specs=[pl.BlockSpec(memory_space=pltpu.VMEM)] * 3,
        out_specs=(pl.BlockSpec(memory_space=pltpu.VMEM),) * 4,
        scratch_shapes=[
            pltpu.VMEM((3, 5, QUARTERS, ROWS, LANES), f32),
            pltpu.VMEM((5, QUARTERS, ROWS + 8, LANES), f32),
        ],
        compiler_params=pltpu.CompilerParams(vmem_limit_bytes=LIMIT_INNER),
        cost_estimate=pl.CostEstimate(flops=10, bytes_accessed=10, transcendentals=0),
    )(view, stream_a, stream_b)


def field_kernel(
    span_a, span_b, table, _e0, _e1, _der, _tile_of, out, mark, e0, e1, der, e2, gspan, gstream, done, result, sems
):
    odd = lax.axis_index("span") % 2

    def halo_planes(before, after):
        def body(c, _):
            for src, high in ((before, False), (after, True)):
                for distance, row, count, base in REACH:
                    plane = 6 + distance if high else HALO - distance
                    for j in range(QUARTERS):
                        at = (c * QUARTERS + j) * SIDE + base
                        for i in range(0, count, 8):
                            n = min(8, count - i)
                            e0[c, plane, j, pl.ds(HALO + row + i, n), :] = src[pl.ds(at + i, n), :]
            return 0

        lax.fori_loop(0, 5, body, 0)

    @pl.when(odd == 0)
    def _():
        halo_planes(span_b, span_a)

    @pl.when(odd == 1)
    def _():
        halo_planes(span_a, span_b)

    clamp_planes(e0)
    clamp_rows(e0, (1, 2, 7, 8))

    fill, span_faces, outputs = stage_tools(e0, der, gspan, gstream, first_stage(e0, e1))
    wide = chunks_from(1)
    fill(0, MIDDLE)
    fill(9, MIDDLE)

    def prims(i, _):
        fill(jnp.where(i < 2, 1 + i, 5 + i), wide)
        return 0

    lax.fori_loop(0, 4, prims, 0)
    span_faces(0, MIDDLE, 0)
    span_faces(1, wide, 1)
    outputs(1, MIDDLE, True, 0, 1, False)
    span_faces(5, wide, 2)

    def plane_one(i, _):
        p = jnp.where(i < 2, 2 + i, 4 + i)
        high = i & 1
        outputs(p, wide, False, jnp.where(i == 2, 2, 1 - high), high, True)
        return 0

    lax.fori_loop(0, 4, plane_one, 0)
    outputs(8, MIDDLE, True, 1, 0, True)

    def finish_two(c, p, r, i, u, acc):
        e2[c, p, :, pl.ds(r, 8), :] = 0.75 * e0[c, p, :, pl.ds(r, 8), :] + (0.25 * u + 0.0125 * acc)

    clamp_planes(e1)
    clamp_rows(e1, range(2, 8))
    fill, span_faces, outputs = stage_tools(e1, der, gspan, gstream, finish_two)
    wide_two = chunks_from(2)
    fill(1, MIDDLE)
    fill(2, wide_two)
    span_faces(1, MIDDLE, 1)
    fill(3, wide_two)
    span_faces(2, wide_two, 0)
    outputs(2, MIDDLE, True, 1, 0, False)

    def plane_two(p, _):
        fill(p + 1, wide_two)
        outputs(p, wide_two, False, 1 - (p & 1), p & 1, True)
        return 0

    lax.fori_loop(3, 7, plane_two, 0)
    fill(8, MIDDLE)
    outputs(7, MIDDLE, True, 0, 1, True)

    def finish_three(c, p, r, i, u, acc):
        new = (1.0 / 3.0) * e0[c, p, :, pl.ds(r, 8), :] + ((2.0 / 3.0) * u + (0.1 / 3.0) * acc)
        for q in range(QUARTERS):
            done[p - HALO, pl.ds(16 * c + 8 * i, 8), q * LANES : (q + 1) * LANES] = new[q]

    copies = []

    def write(p):
        hi, low = split_bf16(done[p], 2)
        got = lax.dot_general(
            jnp.concatenate([hi, low], axis=0),
            table[...],
            (((1,), (0,)), ((), ())),
            preferred_element_type=f32,
        )
        result[p] = (got[:80] + got[80:]).reshape(5, 16, 512)
        copies.append(pltpu.make_async_copy(result.at[p], out.at[:, p], sems.at[p]))
        copies[-1].start()

    clamp_planes(e2)
    clamp_rows(e2, range(3, 7))
    fill, span_faces, outputs = stage_tools(e2, der, gspan, gstream, finish_three)
    wide_three = chunks_from(3)
    fill(2, MIDDLE)
    fill(3, wide_three)
    span_faces(2, MIDDLE, 0)
    for p in range(3, 7):
        fill(p + 1, wide_three if p < 6 else MIDDLE)
        outputs(p, MIDDLE, True, 1 - (p & 1), p & 1, True)
        if p > 3:
            write(p - HALO - 1)
    write(3)
    mark[...] = jnp.zeros((8, LANES), f32)
    for copy in copies:
        copy.wait()


def advance_field(span_a, span_b, inner, tile_of):
    e0, e1, der, table = inner
    vmem = pl.BlockSpec(memory_space=pltpu.VMEM)
    anywhere = pl.BlockSpec(memory_space=pl.ANY)
    out = pl.pallas_call(
        field_kernel,
        out_shape=(
            jax.ShapeDtypeStruct((5, 4, 16, 512), f32),
            jax.ShapeDtypeStruct((8, LANES), f32),
            jax.ShapeDtypeStruct(e0.shape, f32),
            jax.ShapeDtypeStruct(e1.shape, f32),
            jax.ShapeDtypeStruct(der.shape, f32),
        ),
        in_specs=[vmem] * 6 + [anywhere],
        out_specs=(anywhere,) + (vmem,) * 4,
        input_output_aliases={3: 2, 4: 3, 5: 4},
        scratch_shapes=[
            pltpu.VMEM((5, 10, QUARTERS, ROWS, LANES), f32),
            pltpu.VMEM((3, 5, QUARTERS, ROWS, LANES), f32),
            pltpu.VMEM((5, QUARTERS, ROWS + 8, LANES), f32),
            pltpu.VMEM((4, 80, 512), f32),
            pltpu.VMEM((4, 5, 16, 512), f32),
            pltpu.SemaphoreType.DMA((4,)),
        ],
        compiler_params=pltpu.CompilerParams(vmem_limit_bytes=LIMIT_FIELD),
        cost_estimate=pl.CostEstimate(flops=10, bytes_accessed=10, transcendentals=0),
    )(span_a, span_b, table, e0, e1, der, tile_of)
    return out[0], out[1]


def per_device(state, tiles, volume, surface, height, kelvin):
    view, first, second = view_field(state)
    stream_a, stream_b = swap(first, "stream", 0), swap(second, "stream", 1)

    outgoing = gather_samples(view, volume[0].T)
    received = lax.all_to_all(outgoing, ("span", "stream"), 0, 0, tiled=True)

    first, second = pack_planes(view, stream_b, stream_a, outgoing)
    span_a, span_b = swap(first, "span", 0), swap(second, "span", 1)
    tables = face_tables(tiles, surface[0].T, height.reshape(8, LANES), kelvin.reshape(8, LANES))
    inner = inner_planes(view, stream_a, stream_b)
    field, mark = advance_field(span_a, span_b, inner, tables[1])
    return field, wall_faces(received, tables, mark)


def solution(mesh):
    in_specs = (
        P(None, "span", "stream", None),
        P(("span", "stream")),
        P(("span", "stream"), None, None),
        P(("span", "stream"), None, None),
        P(("span", "stream")),
        P(("span", "stream")),
    )
    out_specs = (P(None, "span", "stream", None), P(None, ("span", "stream")))
    return jax.shard_map(per_device, mesh=mesh, in_specs=in_specs, out_specs=out_specs, check_vma=False)
```

profile of v0, /device:TPU:71, one launch (start us, length us, event | category | flops | bytes accessed | tf_op | source)
XLA Modules:
  0.0 33.4 jit_solution(249030005526506971)
XLA Ops:
  0.6 0.0 copy-start.2
  0.6 0.0 copy-start.1
  0.7 0.0 copy-start
  0.7 1.8 %shard_map.77 = (f32[5,4,4,16,128]{4,3,2,1,0:T(8,128)S(1)}, f32[240,128]{1,0:T(8,128)S(1)}, f32[240,128]{1,0:T(8,128)S(1)}) custom-call(f32[5,4,16,512]{3,2,1,0:T(8,128)} %state.1), custom_call_target="tpu_custom_call" | custom-call | flops 1000000000 | bytes 3000000 | tf_op jit(solution)/shard_map/pallas_call | solution.py:250
  2.5 1.9 %collective-permute-start = (f32[240,128]{1,0:T(8,128)S(1)}, f32[240,128]{1,0:T(8,128)S(1)}, u32[]{:S(2)}, u32[]{:S(2)}) collective-permute-start(f32[240,128]{1,0:T(8,128)S(1)} %get-tuple-element.19), channel_id=1, source_target_pairs={{0,32},{1,2},{2,1},{3,4},{4,3},{5,6},{6,5},{7,8},{8,7},{9,10},{10,... | collective-permute-start | bytes 368648 | tf_op jit(solution)/shard_map/ppermute | solution.py:329
  4.3 0.0 collective-permute-start.1
  4.3 0.7 %copy-done.3 = s32[1,128,8]{1,2,0:T(8,128)S(1)} copy-done((s32[1,128,8]{1,2,0:T(8,128)S(1)}, s32[1,128,8]{1,2,0:T(8,128)}, u32[]{:S(2)}) %copy-start.3) | copy-done | bytes 4120
  5.0 2.2 %shard_map.78._samples = f32[128,128]{1,0:T(8,128)} custom-call(f32[5,4,4,16,128]{4,3,2,1,0:T(8,128)S(1)} %get-tuple-element.18.view, s32[8,128]{1,0:T(8,128)S(1)} %bitcast.16), custom_call_target="tpu_custom_call" | custom-call | flops 1000000000 | bytes 1000000 | tf_op jit(solution)/shard_map/pallas_call | solution.py:67
  7.2 1.8 %collective-permute-done.stream_b = f32[240,128]{1,0:T(8,128)S(1)} collective-permute-done((f32[240,128]{1,0:T(8,128)S(1)}, f32[240,128]{1,0:T(8,128)S(1)}, u32[]{:S(2)}, u32[]{:S(2)}) %collective-permute-start) | collective-permute-done | bytes 122912 | tf_op jit(solution)/shard_map/ppermute | solution.py:329
  9.0 0.0 collective-permute-done.1.stream_a
  9.0 0.1 shard_map.79
  9.1 1.4 %collective-permute-start.2 = (f32[1080,128]{1,0:T(8,128)S(1)}, f32[1080,128]{1,0:T(8,128)S(1)}, u32[]{:S(2)}, u32[]{:S(2)}) collective-permute-start(f32[1080,128]{1,0:T(8,128)S(1)} %get-tuple-element.21), channel_id=1, source_target_pairs={{0,32},{1,33},{2,34},{3,35},{4,36},{5,37},{6,38},{7,39},{8,40},{9,... | collective-permute-start | bytes 1658888 | tf_op jit(solution)/shard_map/ppermute | solution.py:329
  10.5 0.0 collective-permute-start.3
  10.5 9.3 %all-to-all-start = ((f32[128,1,128]{2,1,0:T(1,128)}), f32[128,1,128]{2,1,0:T(1,128)S(1)}, u32[]{:S(2)}, u32[]{:S(2)}) async-start(f32[128,1,128]{2,1,0:T(1,128)} %bitcast.7), calls=%async_computation | async-start | bytes 131072 | tf_op jit(solution)/shard_map/all_to_all | solution.py:693
  20.5 0.0 copy-done.2
  20.5 0.0 copy-done.1
  20.5 0.0 copy-done
  20.6 0.3 shard_map.81
  20.9 1.1 %shard_map.80 = (f32[5,10,4,40,128]{4,3,2,1,0:T(8,128)S(1)}, f32[5,10,4,40,128]{4,3,2,1,0:T(8,128)S(1)}, f32[12,10,4,40,128]{4,3,2,1,0:T(8,128)S(1)}, bf16[512,512]{1,0:T(8,128)(2,1)S(1)}) custom-call(f32[5,4,4,16,128]{4,3,2,1,0:T(8,128)S(1)} %get-tuple-element.18.view, f32[240,128]{1,0:T(8,128)S(1)} %collective-permute-done.1.stream_a, ...), custom_call_target="tpu_custom_call" | custom-call | flops 10 | bytes 10 | tf_op jit(solution)/shard_map/pallas_call | solution.py:525
  22.0 1.1 %collective-permute-done.2.span_a = f32[1080,128]{1,0:T(8,128)S(1)} collective-permute-done((f32[1080,128]{1,0:T(8,128)S(1)}, f32[1080,128]{1,0:T(8,128)S(1)}, u32[]{:S(2)}, u32[]{:S(2)}) %collective-permute-start.2) | collective-permute-done | bytes 552992 | tf_op jit(solution)/shard_map/ppermute | solution.py:329
  23.2 2.1 %collective-permute-done.3.span_b = f32[1080,128]{1,0:T(8,128)S(1)} collective-permute-done((f32[1080,128]{1,0:T(8,128)S(1)}, f32[1080,128]{1,0:T(8,128)S(1)}, u32[]{:S(2)}, u32[]{:S(2)}) %collective-permute-start.3) | collective-permute-done | bytes 552992 | tf_op jit(solution)/shard_map/ppermute | solution.py:329
  25.3 6.5 %shard_map.82 = (f32[5,4,16,512]{3,2,1,0:T(8,128)}, f32[8,128]{1,0:T(8,128)S(1)}, f32[5,10,4,40,128]{4,3,2,1,0:T(8,128)S(1)}, f32[5,10,4,40,128]{4,3,2,1,0:T(8,128)S(1)}, f32[12,10,4,40,128]{4,3,2,1,0:T(8,128)S(1)}) custom-call(f32[1080,128]{1,0:T(8,128)S(1)} %collective-permute-done.2.span_a, ...), custom_call_target="tpu_custom_call", output_to_operand_aliasing={{2}: (3, {}), {3}: (4, {}), {4}: (5, {})} | custom-call | flops 10 | bytes 10 | tf_op jit(solution)/shard_map/pallas_call | solution.py:662
  31.8 0.0 all-to-all-done
  31.8 1.6 %shard_map.83 = f32[2,1024]{1,0:T(2,128)} custom-call(f32[128,128]{1,0:T(8,128)S(1)} %bitcast.12, bf16[1024,128]{1,0:T(8,128)(2,1)S(1)} %get-tuple-element.29.hot, s32[8,128]{1,0:T(8,128)S(1)} %get-tuple-element.27._tile_of.tile_of, f32[8,128]{1,0:T(8,128)S(1)} %get-tuple-element.30.alive, f32[8,128]{1,0:T(8,128)S(1)} %get-tuple-element.31.height, ...), custom_call_target="tpu_custom_call" | custom-call | flops 100000000 | bytes 1000000 | tf_op jit(solution)/shard_map/pallas_call | solution.py:191
  (1 shorter events, 0.0 us)
Async XLA Ops:
  0.6 19.9 %copy-start.2 = (f32[1024]{0:T(1024)S(1)}, f32[1024]{0:T(1024)}, u32[]{:S(2)}) copy-start(f32[1024]{0:T(1024)} %param.11) | copy-start | bytes 12292
  0.6 19.9 %copy-start.1 = (f32[1024]{0:T(1024)S(1)}, f32[1024]{0:T(1024)}, u32[]{:S(2)}) copy-start(f32[1024]{0:T(1024)} %param.10) | copy-start | bytes 12292
  0.7 19.9 %copy-start = (s32[1,128,8]{1,2,0:T(8,128)S(1)}, s32[1,128,8]{1,2,0:T(8,128)}, u32[]{:S(2)}) copy-start(s32[1,128,8]{1,2,0:T(8,128)} %param.9) | copy-start | bytes 12292
  2.5 6.5 %collective-permute-start = (f32[240,128]{1,0:T(8,128)S(1)}, f32[240,128]{1,0:T(8,128)S(1)}, u32[]{:S(2)}, u32[]{:S(2)}) collective-permute-start(f32[240,128]{1,0:T(8,128)S(1)} %get-tuple-element.19), channel_id=1, source_target_pairs={{0,32},{1,2},{2,1},{3,4},{4,3},{5,6},{6,5},{7,8},{8,7},{9,10},{10,... | collective-permute-start | bytes 368648 | tf_op jit(solution)/shard_map/ppermute | solution.py:329
  4.3 4.6 %collective-permute-start.1 = (f32[240,128]{1,0:T(8,128)S(1)}, f32[240,128]{1,0:T(8,128)S(1)}, u32[]{:S(2)}, u32[]{:S(2)}) collective-permute-start(f32[240,128]{1,0:T(8,128)S(1)} %get-tuple-element.20), channel_id=1, source_target_pairs={{0,1},{1,0},{2,3},{3,2},{4,5},{5,4},{6,7},{7,6},{8,9},{9,8},{10,11... | collective-permute-start | bytes 368648 | tf_op jit(solution)/shard_map/ppermute | solution.py:329
  4.3 0.7 %copy-start.3 = (s32[1,128,8]{1,2,0:T(8,128)S(1)}, s32[1,128,8]{1,2,0:T(8,128)}, u32[]{:S(2)}) copy-start(s32[1,128,8]{1,2,0:T(8,128)} %param.8) | copy-start | bytes 12292
  9.1 14.1 %collective-permute-start.2 = (f32[1080,128]{1,0:T(8,128)S(1)}, f32[1080,128]{1,0:T(8,128)S(1)}, u32[]{:S(2)}, u32[]{:S(2)}) collective-permute-start(f32[1080,128]{1,0:T(8,128)S(1)} %get-tuple-element.21), channel_id=1, source_target_pairs={{0,32},{1,33},{2,34},{3,35},{4,36},{5,37},{6,38},{7,39},{8,40},{9,... | collective-permute-start | bytes 1658888 | tf_op jit(solution)/shard_map/ppermute | solution.py:329
  10.5 14.7 %collective-permute-start.3 = (f32[1080,128]{1,0:T(8,128)S(1)}, f32[1080,128]{1,0:T(8,128)S(1)}, u32[]{:S(2)}, u32[]{:S(2)}) collective-permute-start(f32[1080,128]{1,0:T(8,128)S(1)} %get-tuple-element.22), channel_id=1, source_target_pairs={{0,1},{1,0},{2,3},{3,2},{4,5},{5,4},{6,7},{7,6},{8,9},{9,8},{10,11... | collective-permute-start | bytes 1658888 | tf_op jit(solution)/shard_map/ppermute | solution.py:329
  10.5 21.2 %all-to-all-start = ((f32[128,1,128]{2,1,0:T(1,128)}), f32[128,1,128]{2,1,0:T(1,128)S(1)}, u32[]{:S(2)}, u32[]{:S(2)}) async-start(f32[128,1,128]{2,1,0:T(1,128)} %bitcast.7), calls=%async_computation | async-start | bytes 131072 | tf_op jit(solution)/shard_map/all_to_all | solution.py:693
where the time goes:
time: 33.7 us; the launch traced here: 33.4 us
  Pallas kernels  13.7 us (41%)
  starting transfers between devices  12.6 us (37%)
  waiting for transfers between devices  5 us (15%)
  between operations  1.38 us (4%)
  local copies, waits for them, and re-layouts  0.7 us (2%)
    all_to_all x1, starting transfers between devices, per_device(): received = lax.all_to_all(outgoing, ('span', 'stream'), 0, 0, tiled=True)  9.33 us
    pallas_call x1, Pallas kernels, advance_field(): pl.pallas_call(field_kernel, out_shape=(jax.ShapeDtypeStruct((5, 4, 16, 5...  6.48 us
    ppermute x4, waiting for transfers between devices, swap(): return lax.ppermute(x, ('span', 'stream'), pairs)  5 us
    ppermute x4, starting transfers between devices, swap(): return lax.ppermute(x, ('span', 'stream'), pairs)  3.29 us
    pallas_call x1, Pallas kernels, gather_samples(): pl.pallas_call(gather_kernel, out_shape=jax.ShapeDtypeStruct((LANES, LANE...  2.19 us
    pallas_call x1, Pallas kernels, view_field(): pl.pallas_call(view_kernel, out_shape=(jax.ShapeDtypeStruct((5, 4, QUARTE...  1.8 us
    pallas_call x1, Pallas kernels, wall_faces(): pl.pallas_call(wall_kernel, out_shape=jax.ShapeDtypeStruct((2, 8 * LANES)...  1.64 us
    pallas_call x1, Pallas kernels, inner_planes(): pl.pallas_call(inner_kernel, out_shape=(block, block, jax.ShapeDtypeStruc...  1.14 us
  transfers between devices with their start and end apart: 5, of which 3 were waited for; matrix products, arithmetic and copies ran while one was open for 0% of the time, Pallas kernels for 30%

commit v1 on v0

--- a/solution.py
+++ b/solution.py
@@ -155,13 +155,13 @@
 
     def eddy(a, b, j):
         damp = 1.0 - jnp.exp2(b * _middle[j])
-        return (a * _middle[j]) * (damp * damp)
+        return a * (damp * damp)
 
     def step(_, tau):
         a, b = viscosity(tau)
         total = [jnp.zeros_like(tau) for _ in range(4)]
         for j in range(NPTS - 1):
-            total[j % 4] = total[j % 4] + _spacing[j] * inverse(0.002 + eddy(a, b, j))
+            total[j % 4] = total[j % 4] + (_spacing[j] / _middle[j]) * inverse(0.002 / _middle[j] + eddy(a, b, j))
         total = (total[0] + total[1]) + (total[2] + total[3])
         return tau * speed / (tau * h * total)
 
@@ -172,9 +172,9 @@
     work = jnp.zeros_like(tau)
     for j in range(NPTS - 1):
         nu = eddy(a, b, j)
-        increment = _spacing[j] * inverse(0.002 + nu)
+        increment = (_spacing[j] / _middle[j]) * inverse(0.002 / _middle[j] + nu)
         total = total + increment
-        part = _spacing[j] * inverse(3.5 * (0.002 / 0.72) + (3.5 / 0.9) * nu)
+        part = (_spacing[j] / _middle[j] / (3.5 / 0.9)) * inverse((0.9 / 0.72) * 0.002 / _middle[j] + nu)
         impedance = impedance + part
         work = work + (total - 0.5 * increment) * part
     scale = tau * h
@@ -215,22 +215,13 @@
     return got[:320] + got[320:]
 
 
-def view_kernel(state, view, first, second, raw, halves, sems):
-    copies = [
-        [pltpu.make_async_copy(state.at[c, a], raw.at[c, a], sems.at[4 * c + a]) for a in range(4)]
-        for c in range(5)
-    ]
-    for c in range(5):
-        for copy in copies[c]:
-            copy.start()
+def view_kernel(state, view, first, second, halves):
     table = pitch_map(False)
     odd = lax.axis_index("stream") % 2
     row_first = (1 - odd) * (16 - HALO)
     row_second = odd * (16 - HALO)
     for c in range(5):
-        for copy in copies[c]:
-            copy.wait()
-        put_halves(halves, c, raw[c].reshape(64, 512))
+        put_halves(halves, c, state[c].reshape(64, 512))
     x = remap(halves, table)
     for c in range(5):
         for a in range(4):
@@ -250,16 +241,14 @@
     return pl.pallas_call(
         view_kernel,
         out_shape=(jax.ShapeDtypeStruct((5, 4, QUARTERS, 16, LANES), f32), side, side),
-        in_specs=[pl.BlockSpec(memory_space=pltpu.HBM)],
+        in_specs=[pl.BlockSpec(memory_space=pltpu.VMEM)],
         out_specs=(pl.BlockSpec(memory_space=pltpu.VMEM),) * 3,
         scratch_shapes=[
-            pltpu.VMEM((5, 4, 16, 512), f32),
             pltpu.VMEM((640, 512), bf16),
-            pltpu.SemaphoreType.DMA((20,)),
         ],
         compiler_params=pltpu.CompilerParams(vmem_limit_bytes=40 * 2**20),
         cost_estimate=pl.CostEstimate(flops=10**9, bytes_accessed=3 * 10**6, transcendentals=0),
-    )(pltpu.with_memory_space_constraint(state, pltpu.HBM))
+    )(state)
 
 
 REACH = ((1, -2, 20, 0), (2, -1, 18, 20), (3, 0, 16, 38))

time: 33.7 us -> 33.4 us (level)
  Pallas kernels: 13.7 us -> 12.4 us
  local copies, waits for them, and re-layouts: 0.7 us -> 1.79 us
    pallas_call x1, Pallas kernels: 1.8 us -> 0.57 us  [view_field(): pl.pallas_call(view_kernel, out_shape=(jax.ShapeDtypeStruct((5, 4, QUARTE...]
    unnamed x8 -> x10, local copies, waits for them, and re-layouts: 0.7 us -> 1.79 us
where the time goes in v1:
time: 33.4 us; the launch traced here: 33.2 us
  starting transfers between devices  12.6 us (38%)
  Pallas kernels  12.4 us (37%)
  waiting for transfers between devices  5.02 us (15%)
  local copies, waits for them, and re-layouts  1.79 us (5%)
  between operations  1.38 us (4%)
    all_to_all x1, starting transfers between devices, per_device(): received = lax.all_to_all(outgoing, ('span', 'stream'), 0, 0, tiled=True)  9.33 us
    pallas_call x1, Pallas kernels, advance_field(): pl.pallas_call(field_kernel, out_shape=(jax.ShapeDtypeStruct((5, 4, 16, 5...  6.48 us
    ppermute x4, waiting for transfers between devices, swap(): return lax.ppermute(x, ('span', 'stream'), pairs)  5.01 us
    ppermute x4, starting transfers between devices, swap(): return lax.ppermute(x, ('span', 'stream'), pairs)  3.28 us
    pallas_call x1, Pallas kernels, gather_samples(): pl.pallas_call(gather_kernel, out_shape=jax.ShapeDtypeStruct((LANES, LANE...  2.18 us
    unnamed x10, local copies, waits for them, and re-layouts  1.79 us
    pallas_call x1, Pallas kernels, wall_faces(): pl.pallas_call(wall_kernel, out_shape=jax.ShapeDtypeStruct((2, 8 * LANES)...  1.6 us
    pallas_call x1, Pallas kernels, inner_planes(): pl.pallas_call(inner_kernel, out_shape=(block, block, jax.ShapeDtypeStruc...  1.14 us
  transfers between devices with their start and end apart: 5, of which 3 were waited for; matrix products, arithmetic and copies ran while one was open for 0% of the time, Pallas kernels for 30%

profile of v1, /device:TPU:71, one launch (start us, length us, event | category | flops | bytes accessed | tf_op | source)
XLA Modules:
  0.0 33.2 jit_solution(13894211946387660447)
XLA Ops:
  0.6 0.0 copy-start.2
  0.6 0.0 copy-start.1
  0.7 1.1 %copy-done.3 = f32[5,4,16,512]{3,2,1,0:T(8,128)S(1)} copy-done((f32[5,4,16,512]{3,2,1,0:T(8,128)S(1)}, f32[5,4,16,512]{3,2,1,0:T(8,128)}, u32[]{:S(2)}) %copy-start.3) | copy-done | bytes 655384
  1.8 0.6 %shard_map.77 = (f32[5,4,4,16,128]{4,3,2,1,0:T(8,128)S(1)}, f32[240,128]{1,0:T(8,128)S(1)}, f32[240,128]{1,0:T(8,128)S(1)}) custom-call(f32[5,4,16,512]{3,2,1,0:T(8,128)S(1)} %copy-done.3), custom_call_target="tpu_custom_call" | custom-call | flops 1000000000 | bytes 3000000 | tf_op jit(solution)/shard_map/pallas_call | solution.py:241
  2.3 1.9 %collective-permute-start = (f32[240,128]{1,0:T(8,128)S(1)}, f32[240,128]{1,0:T(8,128)S(1)}, u32[]{:S(2)}, u32[]{:S(2)}) collective-permute-start(f32[240,128]{1,0:T(8,128)S(1)} %get-tuple-element.19), channel_id=1, source_target_pairs={{0,32},{1,2},{2,1},{3,4},{4,3},{5,6},{6,5},{7,8},{8,7},{9,10},{10,... | collective-permute-start | bytes 368648 | tf_op jit(solution)/shard_map/ppermute | solution.py:318
  4.2 0.0 collective-permute-start.1
  4.2 0.7 %copy-done.4 = s32[1,128,8]{1,2,0:T(8,128)S(1)} copy-done((s32[1,128,8]{1,2,0:T(8,128)S(1)}, s32[1,128,8]{1,2,0:T(8,128)}, u32[]{:S(2)}) %copy-start.4) | copy-done | bytes 4120
  4.9 2.2 %shard_map.78._samples = f32[128,128]{1,0:T(8,128)} custom-call(f32[5,4,4,16,128]{4,3,2,1,0:T(8,128)S(1)} %get-tuple-element.18.view, s32[8,128]{1,0:T(8,128)S(1)} %bitcast.16), custom_call_target="tpu_custom_call" | custom-call | flops 1000000000 | bytes 1000000 | tf_op jit(solution)/shard_map/pallas_call | solution.py:67
  7.1 1.8 %collective-permute-done.stream_b = f32[240,128]{1,0:T(8,128)S(1)} collective-permute-done((f32[240,128]{1,0:T(8,128)S(1)}, f32[240,128]{1,0:T(8,128)S(1)}, u32[]{:S(2)}, u32[]{:S(2)}) %collective-permute-start) | collective-permute-done | bytes 122912 | tf_op jit(solution)/shard_map/ppermute | solution.py:318
  8.8 0.0 collective-permute-done.1.stream_a
  8.8 0.1 shard_map.79
  9.0 1.4 %collective-permute-start.2 = (f32[1080,128]{1,0:T(8,128)S(1)}, f32[1080,128]{1,0:T(8,128)S(1)}, u32[]{:S(2)}, u32[]{:S(2)}) collective-permute-start(f32[1080,128]{1,0:T(8,128)S(1)} %get-tuple-element.21), channel_id=1, source_target_pairs={{0,32},{1,33},{2,34},{3,35},{4,36},{5,37},{6,38},{7,39},{8,40},{9,... | collective-permute-start | bytes 1658888 | tf_op jit(solution)/shard_map/ppermute | solution.py:318
  10.4 0.0 collective-permute-start.3
  10.4 9.3 %all-to-all-start = ((f32[128,1,128]{2,1,0:T(1,128)}), f32[128,1,128]{2,1,0:T(1,128)S(1)}, u32[]{:S(2)}, u32[]{:S(2)}) async-start(f32[128,1,128]{2,1,0:T(1,128)} %bitcast.7), calls=%async_computation | async-start | bytes 131072 | tf_op jit(solution)/shard_map/all_to_all | solution.py:682
  20.4 0.0 copy-done.2
  20.4 0.0 copy-done.1
  20.4 0.0 copy-done
  20.4 0.3 shard_map.81
  20.8 1.1 %shard_map.80 = (f32[5,10,4,40,128]{4,3,2,1,0:T(8,128)S(1)}, f32[5,10,4,40,128]{4,3,2,1,0:T(8,128)S(1)}, f32[12,10,4,40,128]{4,3,2,1,0:T(8,128)S(1)}, bf16[512,512]{1,0:T(8,128)(2,1)S(1)}) custom-call(f32[5,4,4,16,128]{4,3,2,1,0:T(8,128)S(1)} %get-tuple-element.18.view, f32[240,128]{1,0:T(8,128)S(1)} %collective-permute-done.1.stream_a, ...), custom_call_target="tpu_custom_call" | custom-call | flops 10 | bytes 10 | tf_op jit(solution)/shard_map/pallas_call | solution.py:514
  21.9 1.1 %collective-permute-done.2.span_a = f32[1080,128]{1,0:T(8,128)S(1)} collective-permute-done((f32[1080,128]{1,0:T(8,128)S(1)}, f32[1080,128]{1,0:T(8,128)S(1)}, u32[]{:S(2)}, u32[]{:S(2)}) %collective-permute-start.2) | collective-permute-done | bytes 552992 | tf_op jit(solution)/shard_map/ppermute | solution.py:318
  23.0 2.1 %collective-permute-done.3.span_b = f32[1080,128]{1,0:T(8,128)S(1)} collective-permute-done((f32[1080,128]{1,0:T(8,128)S(1)}, f32[1080,128]{1,0:T(8,128)S(1)}, u32[]{:S(2)}, u32[]{:S(2)}) %collective-permute-start.3) | collective-permute-done | bytes 552992 | tf_op jit(solution)/shard_map/ppermute | solution.py:318
  25.1 6.5 %shard_map.82 = (f32[5,4,16,512]{3,2,1,0:T(8,128)}, f32[8,128]{1,0:T(8,128)S(1)}, f32[5,10,4,40,128]{4,3,2,1,0:T(8,128)S(1)}, f32[5,10,4,40,128]{4,3,2,1,0:T(8,128)S(1)}, f32[12,10,4,40,128]{4,3,2,1,0:T(8,128)S(1)}) custom-call(f32[1080,128]{1,0:T(8,128)S(1)} %collective-permute-done.2.span_a, ...), custom_call_target="tpu_custom_call", output_to_operand_aliasing={{2}: (3, {}), {3}: (4, {}), {4}: (5, {})} | custom-call | flops 10 | bytes 10 | tf_op jit(solution)/shard_map/pallas_call | solution.py:651
  31.6 0.0 all-to-all-done
  31.6 1.6 %shard_map.83 = f32[2,1024]{1,0:T(2,128)} custom-call(f32[128,128]{1,0:T(8,128)S(1)} %bitcast.12, bf16[1024,128]{1,0:T(8,128)(2,1)S(1)} %get-tuple-element.29.hot, s32[8,128]{1,0:T(8,128)S(1)} %get-tuple-element.27._tile_of.tile_of, f32[8,128]{1,0:T(8,128)S(1)} %get-tuple-element.30.alive, f32[8,128]{1,0:T(8,128)S(1)} %get-tuple-element.31.height, ...), custom_call_target="tpu_custom_call" | custom-call | flops 100000000 | bytes 1000000 | tf_op jit(solution)/shard_map/pallas_call | solution.py:191
  (3 shorter events, 0.0 us)
Async XLA Ops:
  0.6 19.8 %copy-start.2 = (f32[1024]{0:T(1024)S(1)}, f32[1024]{0:T(1024)}, u32[]{:S(2)}) copy-start(f32[1024]{0:T(1024)} %param.11) | copy-start | bytes 12292
  0.6 19.8 %copy-start.1 = (f32[1024]{0:T(1024)S(1)}, f32[1024]{0:T(1024)}, u32[]{:S(2)}) copy-start(f32[1024]{0:T(1024)} %param.10) | copy-start | bytes 12292
  0.7 1.1 %copy-start.3 = (f32[5,4,16,512]{3,2,1,0:T(8,128)S(1)}, f32[5,4,16,512]{3,2,1,0:T(8,128)}, u32[]{:S(2)}) copy-start(f32[5,4,16,512]{3,2,1,0:T(8,128)} %state.1) | copy-start | bytes 1966084
  1.8 18.7 %copy-start = (s32[1,128,8]{1,2,0:T(8,128)S(1)}, s32[1,128,8]{1,2,0:T(8,128)}, u32[]{:S(2)}) copy-start(s32[1,128,8]{1,2,0:T(8,128)} %param.9) | copy-start | bytes 12292
  2.3 6.5 %collective-permute-start = (f32[240,128]{1,0:T(8,128)S(1)}, f32[240,128]{1,0:T(8,128)S(1)}, u32[]{:S(2)}, u32[]{:S(2)}) collective-permute-start(f32[240,128]{1,0:T(8,128)S(1)} %get-tuple-element.19), channel_id=1, source_target_pairs={{0,32},{1,2},{2,1},{3,4},{4,3},{5,6},{6,5},{7,8},{8,7},{9,10},{10,... | collective-permute-start | bytes 368648 | tf_op jit(solution)/shard_map/ppermute | solution.py:318
  4.2 4.6 %collective-permute-start.1 = (f32[240,128]{1,0:T(8,128)S(1)}, f32[240,128]{1,0:T(8,128)S(1)}, u32[]{:S(2)}, u32[]{:S(2)}) collective-permute-start(f32[240,128]{1,0:T(8,128)S(1)} %get-tuple-element.20), channel_id=1, source_target_pairs={{0,1},{1,0},{2,3},{3,2},{4,5},{5,4},{6,7},{7,6},{8,9},{9,8},{10,11... | collective-permute-start | bytes 368648 | tf_op jit(solution)/shard_map/ppermute | solution.py:318
  4.2 0.7 %copy-start.4 = (s32[1,128,8]{1,2,0:T(8,128)S(1)}, s32[1,128,8]{1,2,0:T(8,128)}, u32[]{:S(2)}) copy-start(s32[1,128,8]{1,2,0:T(8,128)} %param.8) | copy-start | bytes 12292
  9.0 14.0 %collective-permute-start.2 = (f32[1080,128]{1,0:T(8,128)S(1)}, f32[1080,128]{1,0:T(8,128)S(1)}, u32[]{:S(2)}, u32[]{:S(2)}) collective-permute-start(f32[1080,128]{1,0:T(8,128)S(1)} %get-tuple-element.21), channel_id=1, source_target_pairs={{0,32},{1,33},{2,34},{3,35},{4,36},{5,37},{6,38},{7,39},{8,40},{9,... | collective-permute-start | bytes 1658888 | tf_op jit(solution)/shard_map/ppermute | solution.py:318
  10.4 14.7 %collective-permute-start.3 = (f32[1080,128]{1,0:T(8,128)S(1)}, f32[1080,128]{1,0:T(8,128)S(1)}, u32[]{:S(2)}, u32[]{:S(2)}) collective-permute-start(f32[1080,128]{1,0:T(8,128)S(1)} %get-tuple-element.22), channel_id=1, source_target_pairs={{0,1},{1,0},{2,3},{3,2},{4,5},{5,4},{6,7},{7,6},{8,9},{9,8},{10,11... | collective-permute-start | bytes 1658888 | tf_op jit(solution)/shard_map/ppermute | solution.py:318
  10.4 21.2 %all-to-all-start = ((f32[128,1,128]{2,1,0:T(1,128)}), f32[128,1,128]{2,1,0:T(1,128)S(1)}, u32[]{:S(2)}, u32[]{:S(2)}) async-start(f32[128,1,128]{2,1,0:T(1,128)} %bitcast.7), calls=%async_computation | async-start | bytes 131072 | tf_op jit(solution)/shard_map/all_to_all | solution.py:682

commit v2 on v1

--- a/solution.py
+++ b/solution.py
@@ -585,7 +585,7 @@
     outputs(8, MIDDLE, True, 1, 0, True)
 
     def finish_two(c, p, r, i, u, acc):
-        e2[c, p, :, pl.ds(r, 8), :] = 0.75 * e0[c, p, :, pl.ds(r, 8), :] + (0.25 * u + 0.0125 * acc)
+        e2[c, p, :, pl.ds(r, 8), :] = 3.0 * e0[c, p, :, pl.ds(r, 8), :] + (u + 0.05 * acc)
 
     clamp_planes(e1)
     clamp_rows(e1, range(2, 8))
@@ -608,7 +608,7 @@
     outputs(7, MIDDLE, True, 0, 1, True)
 
     def finish_three(c, p, r, i, u, acc):
-        new = (1.0 / 3.0) * e0[c, p, :, pl.ds(r, 8), :] + ((2.0 / 3.0) * u + (0.1 / 3.0) * acc)
+        new = (1.0 / 3.0) * e0[c, p, :, pl.ds(r, 8), :] + ((0.5 / 3.0) * u + (0.025 / 3.0) * acc)
         for q in range(QUARTERS):
             done[p - HALO, pl.ds(16 * c + 8 * i, 8), q * LANES : (q + 1) * LANES] = new[q]
 

time: 33.4 us -> 33.3 us (level)
  no operation moved by 1% of the time
where the time goes in v2:
time: 33.3 us; the launch traced here: 33.1 us
  starting transfers between devices  12.6 us (38%)
  Pallas kernels  12.3 us (37%)
  waiting for transfers between devices  5.02 us (15%)
  local copies, waits for them, and re-layouts  1.79 us (5%)
  between operations  1.38 us (4%)
    all_to_all x1, starting transfers between devices, per_device(): received = lax.all_to_all(outgoing, ('span', 'stream'), 0, 0, tiled=True)  9.33 us
    pallas_call x1, Pallas kernels, advance_field(): pl.pallas_call(field_kernel, out_shape=(jax.ShapeDtypeStruct((5, 4, 16, 5...  6.33 us
    ppermute x4, waiting for transfers between devices, swap(): return lax.ppermute(x, ('span', 'stream'), pairs)  5.01 us
    ppermute x4, starting transfers between devices, swap(): return lax.ppermute(x, ('span', 'stream'), pairs)  3.28 us
    pallas_call x1, Pallas kernels, gather_samples(): pl.pallas_call(gather_kernel, out_shape=jax.ShapeDtypeStruct((LANES, LANE...  2.18 us
    unnamed x10, local copies, waits for them, and re-layouts  1.79 us
    pallas_call x1, Pallas kernels, wall_faces(): pl.pallas_call(wall_kernel, out_shape=jax.ShapeDtypeStruct((2, 8 * LANES)...  1.6 us
    pallas_call x1, Pallas kernels, inner_planes(): pl.pallas_call(inner_kernel, out_shape=(block, block, jax.ShapeDtypeStruc...  1.14 us
  transfers between devices with their start and end apart: 5, of which 3 were waited for; matrix products, arithmetic and copies ran while one was open for 0% of the time, Pallas kernels for 30%

profile of v2, /device:TPU:71, one launch (start us, length us, event | category | flops | bytes accessed | tf_op | source)
XLA Modules:
  0.0 33.1 jit_solution(12337399589000220764)
XLA Ops:
  0.6 0.0 copy-start.2
  0.6 0.0 copy-start.1
  0.7 1.1 %copy-done.3 = f32[5,4,16,512]{3,2,1,0:T(8,128)S(1)} copy-done((f32[5,4,16,512]{3,2,1,0:T(8,128)S(1)}, f32[5,4,16,512]{3,2,1,0:T(8,128)}, u32[]{:S(2)}) %copy-start.3) | copy-done | bytes 655384
  1.8 0.6 %shard_map.77 = (f32[5,4,4,16,128]{4,3,2,1,0:T(8,128)S(1)}, f32[240,128]{1,0:T(8,128)S(1)}, f32[240,128]{1,0:T(8,128)S(1)}) custom-call(f32[5,4,16,512]{3,2,1,0:T(8,128)S(1)} %copy-done.3), custom_call_target="tpu_custom_call" | custom-call | flops 1000000000 | bytes 3000000 | tf_op jit(solution)/shard_map/pallas_call | solution.py:241
  2.3 1.9 %collective-permute-start = (f32[240,128]{1,0:T(8,128)S(1)}, f32[240,128]{1,0:T(8,128)S(1)}, u32[]{:S(2)}, u32[]{:S(2)}) collective-permute-start(f32[240,128]{1,0:T(8,128)S(1)} %get-tuple-element.19), channel_id=1, source_target_pairs={{0,32},{1,2},{2,1},{3,4},{4,3},{5,6},{6,5},{7,8},{8,7},{9,10},{10,... | collective-permute-start | bytes 368648 | tf_op jit(solution)/shard_map/ppermute | solution.py:318
  4.2 0.0 collective-permute-start.1
  4.2 0.7 %copy-done.4 = s32[1,128,8]{1,2,0:T(8,128)S(1)} copy-done((s32[1,128,8]{1,2,0:T(8,128)S(1)}, s32[1,128,8]{1,2,0:T(8,128)}, u32[]{:S(2)}) %copy-start.4) | copy-done | bytes 4120
  4.9 2.2 %shard_map.78._samples = f32[128,128]{1,0:T(8,128)} custom-call(f32[5,4,4,16,128]{4,3,2,1,0:T(8,128)S(1)} %get-tuple-element.18.view, s32[8,128]{1,0:T(8,128)S(1)} %bitcast.16), custom_call_target="tpu_custom_call" | custom-call | flops 1000000000 | bytes 1000000 | tf_op jit(solution)/shard_map/pallas_call | solution.py:67
  7.1 1.8 %collective-permute-done.stream_b = f32[240,128]{1,0:T(8,128)S(1)} collective-permute-done((f32[240,128]{1,0:T(8,128)S(1)}, f32[240,128]{1,0:T(8,128)S(1)}, u32[]{:S(2)}, u32[]{:S(2)}) %collective-permute-start) | collective-permute-done | bytes 122912 | tf_op jit(solution)/shard_map/ppermute | solution.py:318
  8.8 0.0 collective-permute-done.1.stream_a
  8.8 0.1 shard_map.79
  9.0 1.4 %collective-permute-start.2 = (f32[1080,128]{1,0:T(8,128)S(1)}, f32[1080,128]{1,0:T(8,128)S(1)}, u32[]{:S(2)}, u32[]{:S(2)}) collective-permute-start(f32[1080,128]{1,0:T(8,128)S(1)} %get-tuple-element.21), channel_id=1, source_target_pairs={{0,32},{1,33},{2,34},{3,35},{4,36},{5,37},{6,38},{7,39},{8,40},{9,... | collective-permute-start | bytes 1658888 | tf_op jit(solution)/shard_map/ppermute | solution.py:318
  10.4 0.0 collective-permute-start.3
  10.4 9.3 %all-to-all-start = ((f32[128,1,128]{2,1,0:T(1,128)}), f32[128,1,128]{2,1,0:T(1,128)S(1)}, u32[]{:S(2)}, u32[]{:S(2)}) async-start(f32[128,1,128]{2,1,0:T(1,128)} %bitcast.7), calls=%async_computation | async-start | bytes 131072 | tf_op jit(solution)/shard_map/all_to_all | solution.py:682
  20.4 0.0 copy-done.2
  20.4 0.0 copy-done.1
  20.4 0.0 copy-done
  20.4 0.3 shard_map.81
  20.8 1.1 %shard_map.80 = (f32[5,10,4,40,128]{4,3,2,1,0:T(8,128)S(1)}, f32[5,10,4,40,128]{4,3,2,1,0:T(8,128)S(1)}, f32[12,10,4,40,128]{4,3,2,1,0:T(8,128)S(1)}, bf16[512,512]{1,0:T(8,128)(2,1)S(1)}) custom-call(f32[5,4,4,16,128]{4,3,2,1,0:T(8,128)S(1)} %get-tuple-element.18.view, f32[240,128]{1,0:T(8,128)S(1)} %collective-permute-done.1.stream_a, ...), custom_call_target="tpu_custom_call" | custom-call | flops 10 | bytes 10 | tf_op jit(solution)/shard_map/pallas_call | solution.py:514
  21.9 1.1 %collective-permute-done.2.span_a = f32[1080,128]{1,0:T(8,128)S(1)} collective-permute-done((f32[1080,128]{1,0:T(8,128)S(1)}, f32[1080,128]{1,0:T(8,128)S(1)}, u32[]{:S(2)}, u32[]{:S(2)}) %collective-permute-start.2) | collective-permute-done | bytes 552992 | tf_op jit(solution)/shard_map/ppermute | solution.py:318
  23.0 2.1 %collective-permute-done.3.span_b = f32[1080,128]{1,0:T(8,128)S(1)} collective-permute-done((f32[1080,128]{1,0:T(8,128)S(1)}, f32[1080,128]{1,0:T(8,128)S(1)}, u32[]{:S(2)}, u32[]{:S(2)}) %collective-permute-start.3) | collective-permute-done | bytes 552992 | tf_op jit(solution)/shard_map/ppermute | solution.py:318
  25.1 6.3 %shard_map.82 = (f32[5,4,16,512]{3,2,1,0:T(8,128)}, f32[8,128]{1,0:T(8,128)S(1)}, f32[5,10,4,40,128]{4,3,2,1,0:T(8,128)S(1)}, f32[5,10,4,40,128]{4,3,2,1,0:T(8,128)S(1)}, f32[12,10,4,40,128]{4,3,2,1,0:T(8,128)S(1)}) custom-call(f32[1080,128]{1,0:T(8,128)S(1)} %collective-permute-done.2.span_a, ...), custom_call_target="tpu_custom_call", output_to_operand_aliasing={{2}: (3, {}), {3}: (4, {}), {4}: (5, {})} | custom-call | flops 10 | bytes 10 | tf_op jit(solution)/shard_map/pallas_call | solution.py:651
  31.5 0.0 all-to-all-done
  31.5 1.6 %shard_map.83 = f32[2,1024]{1,0:T(2,128)} custom-call(f32[128,128]{1,0:T(8,128)S(1)} %bitcast.12, bf16[1024,128]{1,0:T(8,128)(2,1)S(1)} %get-tuple-element.29.hot, s32[8,128]{1,0:T(8,128)S(1)} %get-tuple-element.27._tile_of.tile_of, f32[8,128]{1,0:T(8,128)S(1)} %get-tuple-element.30.alive, f32[8,128]{1,0:T(8,128)S(1)} %get-tuple-element.31.height, ...), custom_call_target="tpu_custom_call" | custom-call | flops 100000000 | bytes 1000000 | tf_op jit(solution)/shard_map/pallas_call | solution.py:191
  (3 shorter events, 0.0 us)
Async XLA Ops:
  0.6 19.8 %copy-start.2 = (f32[1024]{0:T(1024)S(1)}, f32[1024]{0:T(1024)}, u32[]{:S(2)}) copy-start(f32[1024]{0:T(1024)} %param.11) | copy-start | bytes 12292
  0.6 19.8 %copy-start.1 = (f32[1024]{0:T(1024)S(1)}, f32[1024]{0:T(1024)}, u32[]{:S(2)}) copy-start(f32[1024]{0:T(1024)} %param.10) | copy-start | bytes 12292
  0.7 1.1 %copy-start.3 = (f32[5,4,16,512]{3,2,1,0:T(8,128)S(1)}, f32[5,4,16,512]{3,2,1,0:T(8,128)}, u32[]{:S(2)}) copy-start(f32[5,4,16,512]{3,2,1,0:T(8,128)} %state.1) | copy-start | bytes 1966084
  1.8 18.7 %copy-start = (s32[1,128,8]{1,2,0:T(8,128)S(1)}, s32[1,128,8]{1,2,0:T(8,128)}, u32[]{:S(2)}) copy-start(s32[1,128,8]{1,2,0:T(8,128)} %param.9) | copy-start | bytes 12292
  2.3 6.5 %collective-permute-start = (f32[240,128]{1,0:T(8,128)S(1)}, f32[240,128]{1,0:T(8,128)S(1)}, u32[]{:S(2)}, u32[]{:S(2)}) collective-permute-start(f32[240,128]{1,0:T(8,128)S(1)} %get-tuple-element.19), channel_id=1, source_target_pairs={{0,32},{1,2},{2,1},{3,4},{4,3},{5,6},{6,5},{7,8},{8,7},{9,10},{10,... | collective-permute-start | bytes 368648 | tf_op jit(solution)/shard_map/ppermute | solution.py:318
  4.2 4.6 %collective-permute-start.1 = (f32[240,128]{1,0:T(8,128)S(1)}, f32[240,128]{1,0:T(8,128)S(1)}, u32[]{:S(2)}, u32[]{:S(2)}) collective-permute-start(f32[240,128]{1,0:T(8,128)S(1)} %get-tuple-element.20), channel_id=1, source_target_pairs={{0,1},{1,0},{2,3},{3,2},{4,5},{5,4},{6,7},{7,6},{8,9},{9,8},{10,11... | collective-permute-start | bytes 368648 | tf_op jit(solution)/shard_map/ppermute | solution.py:318
  4.2 0.7 %copy-start.4 = (s32[1,128,8]{1,2,0:T(8,128)S(1)}, s32[1,128,8]{1,2,0:T(8,128)}, u32[]{:S(2)}) copy-start(s32[1,128,8]{1,2,0:T(8,128)} %param.8) | copy-start | bytes 12292
  9.0 14.0 %collective-permute-start.2 = (f32[1080,128]{1,0:T(8,128)S(1)}, f32[1080,128]{1,0:T(8,128)S(1)}, u32[]{:S(2)}, u32[]{:S(2)}) collective-permute-start(f32[1080,128]{1,0:T(8,128)S(1)} %get-tuple-element.21), channel_id=1, source_target_pairs={{0,32},{1,33},{2,34},{3,35},{4,36},{5,37},{6,38},{7,39},{8,40},{9,... | collective-permute-start | bytes 1658888 | tf_op jit(solution)/shard_map/ppermute | solution.py:318
  10.4 14.7 %collective-permute-start.3 = (f32[1080,128]{1,0:T(8,128)S(1)}, f32[1080,128]{1,0:T(8,128)S(1)}, u32[]{:S(2)}, u32[]{:S(2)}) collective-permute-start(f32[1080,128]{1,0:T(8,128)S(1)} %get-tuple-element.22), channel_id=1, source_target_pairs={{0,1},{1,0},{2,3},{3,2},{4,5},{5,4},{6,7},{7,6},{8,9},{9,8},{10,11... | collective-permute-start | bytes 1658888 | tf_op jit(solution)/shard_map/ppermute | solution.py:318
  10.4 21.1 %all-to-all-start = ((f32[128,1,128]{2,1,0:T(1,128)}), f32[128,1,128]{2,1,0:T(1,128)S(1)}, u32[]{:S(2)}, u32[]{:S(2)}) async-start(f32[128,1,128]{2,1,0:T(1,128)} %bitcast.7), calls=%async_computation | async-start | bytes 131072 | tf_op jit(solution)/shard_map/all_to_all | solution.py:682
